TPU v7x, 256 devices: a whole 4x4x8 slice. The times are simulated.
256 devices in a mesh: dp: 128 (over x_lo, z, y, core), rows: 2 (over x_hi).
Axes of the slice: x: 4 (x_hi: 2, x_lo: 2; x = x_hi * 2 + x_lo), y: 4, z: 8, core: 2. Of those that a mesh axis runs over, the one named last changes fastest.
Arguments:
- latents: bfloat16 [128, 4, 128, 320], P('dp', 'rows'), may hold values from -6 to 6
- mean_one: float32 [128, 32], P('dp'), may hold values from -0.5 to 0.5
- rstd_one: float32 [128, 32], P('dp'), may hold values from 0.5 to 2
- gain_one: float32 [320], replicated, may hold values from 0.25 to 1.75
- shift_one: float32 [320], replicated, may hold values from -0.5 to 0.5
- kernel_one: bfloat16 [4, 9, 25600], P(None, None, 'dp'), may hold values from -0.109375 to 0.109375
- bias_one: float32 [320], replicated, may hold values from -3 to 3
- embed_bias: float32 [128, 320], P('dp'), may hold values from -3 to 3
- mean_two: float32 [128, 32], P('dp'), may hold values from -0.5 to 0.5
- rstd_two: float32 [128, 32], P('dp'), may hold values from 0.5 to 2
- gain_two: float32 [320], replicated, may hold values from 0.25 to 1.75
- shift_two: float32 [320], replicated, may hold values from -0.5 to 0.5
- kernel_two: bfloat16 [4, 9, 25600], P(None, None, 'dp'), may hold values from -0.109375 to 0.109375
- bias_two: float32 [320], replicated, may hold values from -3 to 3
Outputs:
- block_out: bfloat16 [128, 4, 128, 320], P('dp', 'rows')
All inputs are finite; a program needn't handle non-finite values.
Results may differ from a plain program's by a relative error of at most 0.0045.
Values may be sent and summed in bfloat16 or wider, within the bound.
A program may use at most 192 MiB of HBM per device.

v0:
```python
from functools import partial

import jax
import jax.numpy as jnp
from jax import lax
from jax.sharding import PartitionSpec as P


def padded_2(array, sides, width):
    for axis, dim in sides:
        devices, length = (lax.axis_size(axis), array.shape[dim])
        up = [(i, (i + 1) % devices) for i in range(devices - 1)]
        down = [(j, i) for i, j in up]
        last = lax.slice_in_dim(array, length - width, length, axis=dim)
        first = lax.slice_in_dim(array, 0, width, axis=dim)
        before = lax.ppermute(last, axis, up)
        after = lax.ppermute(first, axis, down)
        array = jnp.concatenate([before, array, after], axis=dim)
    return array


def norm_silu(values, group_mean, group_rstd, gain_vec, shift_vec):
    height, columns, channels = values.shape
    groups = group_mean.shape[-1]
    grouped = values.reshape(height, columns, groups, channels // groups)
    scaled = (grouped - group_mean[0][:, None]) * group_rstd[0][:, None]
    return jax.nn.silu(scaled.reshape(height, columns, channels) * gain_vec + shift_vec)


def padded_rows(activation):
    padded = padded_2(activation, (("rows", 0),), 1)
    return jnp.pad(padded, ((0, 0), (1, 1), (0, 0)))


def window_at(padded, position, height, columns, first_channel, depth):
    tap_row = position // 3
    tap_col = position % 3
    window = padded[
        tap_row : tap_row + height,
        tap_col : tap_col + columns,
        first_channel : first_channel + depth,
    ]
    return window.reshape(height * columns, depth)


def convolve_blocks(activation, kernel, blocks):
    height, columns, channels = activation.shape
    padded = padded_rows(activation)
    accumulated = jnp.zeros((height * columns, channels), jnp.float32)
    for number in range(blocks):
        gathered = lax.all_gather(kernel[number], "dp", axis=1, tiled=True)
        depth = gathered.shape[1] // channels
        weights = gathered.reshape(9 * depth, channels)
        windows = jnp.concatenate(
            [
                window_at(padded, position, height, columns, number * depth, depth)
                for position in range(9)
            ],
            axis=1,
        )
        accumulated = accumulated + jnp.dot(windows, weights, preferred_element_type=jnp.float32)
    return accumulated.reshape(height, columns, channels)


def shards(
    latents,
    mean_one,
    rstd_one,
    gain_one,
    shift_one,
    kernel_one,
    bias_one,
    embed_bias,
    mean_two,
    rstd_two,
    gain_two,
    shift_two,
    kernel_two,
    bias_two,
):
    blocks = kernel_one.shape[0]
    sample = latents[0].astype(jnp.float32)
    first_act = norm_silu(sample, mean_one, rstd_one, gain_one, shift_one).astype(jnp.bfloat16)
    conv_one = partial(convolve_blocks, kernel=kernel_one, blocks=blocks)
    conv_two = partial(convolve_blocks, kernel=kernel_two, blocks=blocks)
    hidden = conv_one(first_act) + bias_one + embed_bias[0]
    second_act = norm_silu(hidden, mean_two, rstd_two, gain_two, shift_two).astype(jnp.bfloat16)
    result = conv_two(second_act) + bias_two + sample
    return result.astype(jnp.bfloat16)[None]


def solution(mesh):
    placed = (
        P("dp", "rows", None, None),
        P("dp", None),
        P("dp", None),
        P(),
        P(),
        P(None, None, "dp"),
        P(),
        P("dp", None),
        P("dp", None),
        P("dp", None),
        P(),
        P(),
        P(None, None, "dp"),
        P(),
    )
    return jax.shard_map(
        shards, mesh=mesh, in_specs=placed, out_specs=P("dp", "rows", None, None), check_vma=False
    )
```

profile of v0, /device:TPU:1, one launch (start us, length us, event | category | flops | bytes accessed | tf_op | source)
XLA Modules:
  0.0 1813.3 jit_solution(14008691890563570396)
XLA Ops:
  0.0 0.7 mul.54
  0.8 0.7 sub.31
  1.7 1.2 fusion.16
  2.9 0.6 fusion.28
  3.5 5.5 collective-permute-start
  9.0 1.3 collective-permute-start.1
  10.3 0.9 fusion.30
  11.4 205.4 %all-gather = bf16[1,9,25600]{1,0,2:T(2,128)(2,1)} all-gather(bf16[1,9,200]{1,0,2:T(2,128)(2,1)S(1)} %copy.181), channel_id=2, replica_groups=mesh['dp'=128,'rows'=2] {'dp'}, dimensions={2}, use_global_device_ids=true | all-gather | bytes 464400 | tf_op jit(solution)/shard_map/all_gather | solution.py:51
  216.9 197.2 %all-gather.1 = bf16[1,9,25600]{1,0,2:T(2,128)(2,1)} all-gather(bf16[1,9,200]{1,0,2:T(2,128)(2,1)S(1)} %copy.182), channel_id=3, replica_groups=mesh['dp'=128,'rows'=2] {'dp'}, dimensions={2}, use_global_device_ids=true | all-gather | bytes 464400 | tf_op jit(solution)/shard_map/all_gather | solution.py:51
  414.2 198.3 %all-gather.2 = bf16[1,9,25600]{1,0,2:T(2,128)(2,1)} all-gather(bf16[1,9,200]{1,0,2:T(2,128)(2,1)S(1)} %copy.183), channel_id=4, replica_groups=mesh['dp'=128,'rows'=2] {'dp'}, dimensions={2}, use_global_device_ids=true | all-gather | bytes 464400 | tf_op jit(solution)/shard_map/all_gather | solution.py:51
  612.6 197.2 %all-gather.3 = bf16[1,9,25600]{1,0,2:T(2,128)(2,1)} all-gather(bf16[1,9,200]{1,0,2:T(2,128)(2,1)S(1)} %copy.184), channel_id=5, replica_groups=mesh['dp'=128,'rows'=2] {'dp'}, dimensions={2}, use_global_device_ids=true | all-gather | bytes 464400 | tf_op jit(solution)/shard_map/all_gather | solution.py:51
  810.0 198.3 %all-gather.4 = bf16[1,9,25600]{1,0,2:T(2,128)(2,1)} all-gather(bf16[1,9,200]{1,0,2:T(2,128)(2,1)S(1)} %copy.185), channel_id=6, replica_groups=mesh['dp'=128,'rows'=2] {'dp'}, dimensions={2}, use_global_device_ids=true | all-gather | bytes 464400 | tf_op jit(solution)/shard_map/all_gather | solution.py:51
  1008.4 197.2 %all-gather.5 = bf16[1,9,25600]{1,0,2:T(2,128)(2,1)} all-gather(bf16[1,9,200]{1,0,2:T(2,128)(2,1)S(1)} %copy.186), channel_id=7, replica_groups=mesh['dp'=128,'rows'=2] {'dp'}, dimensions={2}, use_global_device_ids=true | all-gather | bytes 464400 | tf_op jit(solution)/shard_map/all_gather | solution.py:51
  1205.8 198.4 %all-gather.6 = bf16[1,9,25600]{1,0,2:T(2,128)(2,1)} all-gather(bf16[1,9,200]{1,0,2:T(2,128)(2,1)S(1)} %copy.187), channel_id=8, replica_groups=mesh['dp'=128,'rows'=2] {'dp'}, dimensions={2}, use_global_device_ids=true | all-gather | bytes 464400 | tf_op jit(solution)/shard_map/all_gather | solution.py:51
  1404.2 23.7 %copy.101 = bf16[1,9,25600]{2,1,0:T(8,128)(2,1)S(1)} copy(bf16[1,9,25600]{1,0,2:T(2,128)(2,1)} %all-gather) | data formatting | bytes 921600 | tf_op jit(solution)/shard_map/all_gather | solution.py:51
  1427.9 0.5 reshape.298
  1428.4 23.7 %copy.112 = bf16[1,9,25600]{2,1,0:T(8,128)(2,1)S(1)} copy(bf16[1,9,25600]{1,0,2:T(2,128)(2,1)} %all-gather.1) | data formatting | bytes 921600 | tf_op jit(solution)/shard_map/all_gather | solution.py:51
  1452.6 23.7 %copy.123 = bf16[1,9,25600]{2,1,0:T(8,128)(2,1)S(1)} copy(bf16[1,9,25600]{1,0,2:T(2,128)(2,1)} %all-gather.2) | data formatting | bytes 921600 | tf_op jit(solution)/shard_map/all_gather | solution.py:51
  1476.7 23.7 %copy.134 = bf16[1,9,25600]{2,1,0:T(8,128)(2,1)S(1)} copy(bf16[1,9,25600]{1,0,2:T(2,128)(2,1)} %all-gather.3) | data formatting | bytes 921600 | tf_op jit(solution)/shard_map/all_gather | solution.py:51
  1501.1 0.6 mul.63
  1501.9 0.6 sub.37
  1502.6 0.7 reduce
  1506.6 0.6 fusion.27
  1507.2 6.4 collective-permute-start.2
  1513.6 1.3 collective-permute-start.3
  1514.9 197.7 %all-gather.7 = bf16[1,9,25600]{1,0,2:T(2,128)(2,1)} all-gather(bf16[1,9,200]{1,0,2:T(2,128)(2,1)S(1)} %copy.188), channel_id=9, replica_groups=mesh['dp'=128,'rows'=2] {'dp'}, dimensions={2}, use_global_device_ids=true | all-gather | bytes 464400 | tf_op jit(solution)/shard_map/all_gather | solution.py:51
  1712.6 23.7 %copy.146 = bf16[1,9,25600]{2,1,0:T(8,128)(2,1)S(1)} copy(bf16[1,9,25600]{1,0,2:T(2,128)(2,1)} %all-gather.4) | data formatting | bytes 921600 | tf_op jit(solution)/shard_map/all_gather | solution.py:51
  1736.7 23.7 %copy.157 = bf16[1,9,25600]{2,1,0:T(8,128)(2,1)S(1)} copy(bf16[1,9,25600]{1,0,2:T(2,128)(2,1)} %all-gather.5) | data formatting | bytes 921600 | tf_op jit(solution)/shard_map/all_gather | solution.py:51
  1760.9 23.7 %copy.168 = bf16[1,9,25600]{2,1,0:T(8,128)(2,1)S(1)} copy(bf16[1,9,25600]{1,0,2:T(2,128)(2,1)} %all-gather.6) | data formatting | bytes 921600 | tf_op jit(solution)/shard_map/all_gather | solution.py:51
  1785.1 23.7 %copy.179 = bf16[1,9,25600]{2,1,0:T(8,128)(2,1)S(1)} copy(bf16[1,9,25600]{1,0,2:T(2,128)(2,1)} %all-gather.7) | data formatting | bytes 921600 | tf_op jit(solution)/shard_map/all_gather | solution.py:51
  1808.7 0.5 reshape.369
  1812.6 0.8 fusion.17
  (133 shorter events, 10.4 us)
Async XLA Ops:
  3.5 1499.8 %collective-permute-start = (bf16[1,128,320]{1,2,0:T(8,128)(2,1)}, bf16[1,128,320]{1,2,0:T(8,128)(2,1)S(1)}, u32[]{:S(2)}, u32[]{:S(2)}) collective-permute-start(bf16[1,128,320]{1,2,0:T(8,128)(2,1)} %get-tuple-element.79), channel_id=1, source_target_pairs={{0,1},{2,3},{4,5},{6,7},{8,9},{10,11},{12,13},{14,15},{16,17},{18,... | collective-permute-start | bytes 245768 | tf_op jit(solution)/shard_map/ppermute | solution.py:16
  9.0 1494.4 %collective-permute-start.1 = (bf16[1,128,320]{1,2,0:T(8,128)(2,1)S(1)}, bf16[1,128,320]{1,2,0:T(8,128)(2,1)S(1)}, u32[]{:S(2)}, u32[]{:S(2)}) collective-permute-start(bf16[1,128,320]{1,2,0:T(8,128)(2,1)S(1)} %get-tuple-element.80), channel_id=1, source_target_pairs={{1,0},{3,2},{5,4},{7,6},{9,8},{11,10},{13,12},{15,14},{17,16},{19,... | collective-permute-start | bytes 245768 | tf_op jit(solution)/shard_map/ppermute | solution.py:17
  612.6 197.2 %copy-start.1 = (bf16[4,9,200]{2,0,1:T(4,128)(2,1)S(1)}, bf16[4,9,200]{2,0,1:T(4,128)(2,1)}, u32[]{:S(2)}) copy-start(bf16[4,9,200]{2,0,1:T(4,128)(2,1)} %param.26) | copy-start | bytes 43204
  1500.4 0.7 copy-start.8
  1500.4 1.4 copy-start.9
  1505.3 0.9 copy-start.2
  1505.3 0.9 copy-start.3
  1505.3 0.9 copy-start.4
  1505.3 0.9 copy-start.5
  1505.4 0.9 copy-start.6
  1507.2 302.0 %collective-permute-start.2 = (bf16[1,128,320]{1,2,0:T(8,128)(2,1)}, bf16[1,128,320]{1,2,0:T(8,128)(2,1)S(1)}, u32[]{:S(2)}, u32[]{:S(2)}) collective-permute-start(bf16[1,128,320]{1,2,0:T(8,128)(2,1)} %get-tuple-element.73), channel_id=1, source_target_pairs={{0,1},{2,3},{4,5},{6,7},{8,9},{10,11},{12,13},{14,15},{16,17},{18,... | collective-permute-start | bytes 245768 | tf_op jit(solution)/shard_map/ppermute | solution.py:16
  1513.6 295.7 %collective-permute-start.3 = (bf16[1,128,320]{1,2,0:T(8,128)(2,1)S(1)}, bf16[1,128,320]{1,2,0:T(8,128)(2,1)S(1)}, u32[]{:S(2)}, u32[]{:S(2)}) collective-permute-start(bf16[1,128,320]{1,2,0:T(8,128)(2,1)S(1)} %get-tuple-element.74), channel_id=1, source_target_pairs={{1,0},{3,2},{5,4},{7,6},{9,8},{11,10},{13,12},{15,14},{17,16},{19,... | collective-permute-start | bytes 245768 | tf_op jit(solution)/shard_map/ppermute | solution.py:17
  1811.6 0.9 copy-start
  1811.7 0.9 copy-start.7
where the time goes:
time: 1820 us; the launch traced here: 1810 us
  blocking collectives  1590 us (87%)
  local copies, waits for them, and re-layouts  201 us (11%)
    all_gather x8, blocking collectives, convolve_blocks(): gathered = lax.all_gather(kernel[number], 'dp', axis=1, tiled=True)  1590 us
    all_gather x8, local copies, waits for them, and re-layouts, convolve_blocks(): gathered = lax.all_gather(kernel[number], 'dp', axis=1, tiled=True)  189 us
  transfers between devices with their start and end apart: 4, of which 0 were waited for; matrix products, arithmetic and copies ran while one was open for 11% of the time, Pallas kernels for 0%

commit v1 on v0

v1 whole, which is shorter than its diff:
```python
from functools import partial

import jax
import jax.numpy as jnp
from jax import lax
from jax.experimental import pallas as pl
from jax.experimental.pallas import tpu as pltpu
from jax.sharding import PartitionSpec as P

MESH = pl.DeviceIdType.MESH
BF = jnp.bfloat16
F32 = jnp.float32
Z_STEPS = (1, -1, 2, -2, 3, -3, 4)
Y_STEPS = (1, -1, 2)
SWAPS = tuple((a, b) for a in range(4) for b in range(2) if (a, b) != (0, 0))
SLOT = 128


def device(x, y, z, c):
    x, y, z, c = x % 4, y % 4, z % 8, c % 2
    return ((((x % 2) * 8 + z) * 4 + y) * 2 + c, x // 2)


def silu_norm(values, mean, rstd, gain, shift):
    scaled = ((values - mean) * rstd) * gain + shift
    return scaled / (1.0 + jnp.exp(-scaled))


def spread(channel_values):
    group = lax.broadcasted_iota(jnp.int32, (32, 320), 0)
    lane = lax.broadcasted_iota(jnp.int32, (32, 320), 1)
    pick = jnp.where(lane // 10 == group, 1.0, 0.0).astype(F32)
    wide = jnp.broadcast_to(channel_values, (8, 32))
    return jnp.dot(wide, pick, precision=lax.Precision.HIGHEST, preferred_element_type=F32)[0:1]


def expand(act, pick, tap_lane):
    wide = jnp.dot(act, pick, preferred_element_type=F32)
    row = lax.broadcasted_iota(jnp.int32, (128, 1024), 0)
    before = jnp.where(row == 0, 0.0, pltpu.roll(wide, 1, 0))
    after = jnp.where(row == 127, 0.0, pltpu.roll(wide, 127, 0))
    return jnp.where(tap_lane < 5, before, jnp.where(tap_lane < 10, wide, after)).astype(BF)


def kernel(
    lat_ref, mean1, rstd1, gain1, shift1, k1_ref, bias1, embed, mean2, rstd2, gain2, shift2, k2_ref, bias2,
    out_ref,
    lat, msg, got, held, lhs, sample, pick, acc,
    lat_send, lat_recv, swap_send, swap_recv, z_send, z_recv, y_send, y_recv, x_send, x_recv, c_send, c_recv, local_sem,
):
    d = lax.axis_index("dp")
    h = lax.axis_index("rows")
    c = d % 2
    y = (d // 2) % 4
    z = (d // 8) % 8
    xl = d // 64
    x = 2 * h + xl

    barrier = pltpu.get_barrier_semaphore()
    partners = [device(x, y - a, z, c - b) for a, b in SWAPS]
    partners += [device(x, y, z - s, c) for s in Z_STEPS]
    partners += [device(x + s, y, z, c) for s in (1, 2, 3)]
    for partner in partners:
        pl.semaphore_signal(barrier, inc=1, device_id=partner, device_id_type=MESH)

    own_lat = pltpu.make_async_copy(lat_ref, lat.at[h], local_sem)
    own_lat.start()

    msg[...] = jnp.zeros_like(msg)
    for number, ref in enumerate((k1_ref, k2_ref)):
        raw = ref[...].astype(F32)
        for b in range(4):
            msg[b, number, 0:9, 0:200] = raw[:, b, :].astype(BF)

    lane = lax.broadcasted_iota(jnp.int32, (320, 1024), 1)
    channel = lax.broadcasted_iota(jnp.int32, (320, 1024), 0)
    group = lane // 16
    within = lane % 16
    wanted = (group % 4) * 80 + (group // 4) * 5 + within % 5
    pick[...] = jnp.where((wanted == channel) & (within < 15), 1.0, 0.0).astype(BF)

    pl.semaphore_wait(barrier, len(partners))

    swaps = []
    q = 2 * y + c
    for i, (a, b) in enumerate(SWAPS):
        to_y = (y + a) % 4
        copy = pltpu.make_async_remote_copy(
            src_ref=msg.at[to_y], dst_ref=got.at[q], send_sem=swap_send.at[i], recv_sem=swap_recv.at[i],
            device_id=device(x, y + a, z, c + b), device_id_type=MESH)
        copy.start()
        swaps.append(copy)
    lat_copy = pltpu.make_async_remote_copy(
        src_ref=lat_ref, dst_ref=lat.at[h], send_sem=lat_send, recv_sem=lat_recv,
        device_id=device(x + 2, y, z, c), device_id_type=MESH)
    lat_copy.start()
    got[q] = msg[y]

    for copy in swaps:
        copy.wait()

    col = lax.broadcasted_iota(jnp.int32, (16, 384), 1)
    row48 = lax.broadcasted_iota(jnp.int32, (48, 80), 0)
    col80 = lax.broadcasted_iota(jnp.int32, (48, 80), 1)
    in_tile = row48 % 16
    source = (in_tile % 5) * 16 + (row48 // 16) * 3 + in_tile // 5
    place = jnp.where((source == col80) & (in_tile < 15), 1.0, 0.0).astype(BF)
    whole = []
    for number in range(2):
        pieces = [
            jnp.concatenate([got[i, number].astype(F32), jnp.zeros((16, 128), F32)], axis=1) for i in range(8)
        ]
        rows = []
        for p in range(5):
            total = jnp.zeros((16, 384), F32)
            for i in range(8):
                by = 200 * i - 320 * p
                low, high = max(0, -by), min(200, 320 - by)
                if low < high:
                    part = jnp.where((col >= low) & (col < high), pieces[i], 0.0)
                    total = total + (pltpu.roll(part, by % 384, 1) if by % 384 else part)
            rows.append(total)
        stacked = jnp.concatenate(rows, axis=0).astype(BF)
        whole.append(jnp.dot(place, stacked, preferred_element_type=F32))
    one, two = whole
    slot = (xl * 8 + z) * 4 + y
    first = c == 0
    held[c, slot, 0:48] = jnp.where(first, one[:, 0:128], one[:, 128:256]).astype(BF)
    held[c, slot, 80:128] = jnp.where(first, two[:, 0:128], two[:, 128:256]).astype(BF)
    last = one[:, 256:384] + pltpu.roll(two[:, 256:384], 64, 1)
    held[c, slot, 48:80] = jnp.where(first, last[0:32], last[16:48]).astype(BF)

    copies = []
    for i, s in enumerate(Z_STEPS):
        copy = pltpu.make_async_remote_copy(
            src_ref=held.at[c, slot], dst_ref=held.at[c, slot], send_sem=z_send.at[i], recv_sem=z_recv.at[i],
            device_id=device(x, y, z + s, c), device_id_type=MESH)
        copy.start()
        copies.append(copy)

    own_lat.wait()
    lat_copy.wait()
    m1, r1 = spread(mean1[...]), spread(rstd1[...])
    tap_lane = lax.broadcasted_iota(jnp.int32, (128, 1024), 1) % 16
    g1, s1 = gain1[...].reshape(1, 320), shift1[...].reshape(1, 320)
    lhs[0] = jnp.zeros((128, 1024), BF)
    lhs[5] = jnp.zeros((128, 1024), BF)
    for r in range(4):
        values = lat[r // 2, r % 2].astype(F32).T
        sample[r] = values
        lhs[r + 1] = expand(silu_norm(values, m1, r1, g1, s1).astype(BF), pick[...], tap_lane)

    for copy in copies:
        copy.wait()
    copies = []
    for i, s in enumerate(Y_STEPS):
        for zz in range(8):
            place_of = (xl * 8 + zz) * 4 + y
            copy = pltpu.make_async_remote_copy(
                src_ref=held.at[c, place_of], dst_ref=held.at[c, place_of],
                send_sem=y_send.at[i, zz], recv_sem=y_recv.at[i, zz],
                device_id=device(x, y + s, z, c), device_id_type=MESH)
            copy.start()
            copies.append(copy)
    for copy in copies:
        copy.wait()
    copies = []
    half = pl.ds(xl * 32 + h * 16, 16)
    for i, s in enumerate((1, -1)):
        copy = pltpu.make_async_remote_copy(
            src_ref=held.at[c, half], dst_ref=held.at[c, half], send_sem=x_send.at[i], recv_sem=x_recv.at[i],
            device_id=device(x + s, y, z, c), device_id_type=MESH)
        copy.start()
        copies.append(copy)
    for copy in copies:
        copy.wait()
    copy = pltpu.make_async_remote_copy(
        src_ref=held.at[c], dst_ref=held.at[c], send_sem=c_send, recv_sem=c_recv,
        device_id=device(x, y, z, c + 1), device_id_type=MESH)
    copy.start()
    copy.wait()

    def weights(dy, base):
        t0 = held[0, :, base + 16 * dy : base + 16 * dy + 16].reshape(1024, 128)
        t1 = held[1, :, base + 16 * dy : base + 16 * dy + 16].reshape(1024, 128)
        owner, at = ((0, 48), (0, 64), (1, 64))[dy]
        t2 = held[owner, :, at : at + 16].reshape(1024, 128)
        return jnp.concatenate([t0, t1, t2], axis=1)

    for dy in range(3):
        left = lhs[pl.ds(h + dy, 3)].reshape(384, 1024)
        product = jnp.dot(left, weights(dy, 0), preferred_element_type=F32)
        if dy:
            acc[...] += product
        else:
            acc[...] = product

    m2, r2 = spread(mean2[...]), spread(rstd2[...])
    g2, s2 = gain2[...].reshape(1, 320), shift2[...].reshape(1, 320)
    offset = bias1[...].reshape(1, 320) + embed[...]
    for r in range(3):
        hidden = acc[128 * r : 128 * r + 128, 0:320] + offset
        lhs[r + 1] = expand(silu_norm(hidden, m2, r2, g2, s2).astype(BF), pick[...], tap_lane)
    lhs[4] = jnp.zeros((128, 1024), BF)
    for dy in range(3):
        left = lhs[pl.ds(h + dy, 2)].reshape(256, 1024)
        product = jnp.dot(left, weights(dy, 80), preferred_element_type=F32)
        if dy:
            acc[0:256] += product
        else:
            acc[0:256] = product
    b2 = bias2[...].reshape(1, 320)
    for r in range(2):
        rows = acc[128 * r : 128 * r + 128]
        result = jnp.concatenate([rows[:, 0:256], rows[:, 320:384]], axis=1)
        out_ref[r] = ((result + b2 + sample[2 * h + r]).T).astype(BF)


def shards(latents, mean_one, rstd_one, gain_one, shift_one, kernel_one, bias_one, embed_bias,
           mean_two, rstd_two, gain_two, shift_two, kernel_two, bias_two):
    lat = jnp.transpose(latents[0], (0, 2, 1))
    k1 = jnp.transpose(kernel_one, (1, 0, 2))
    k2 = jnp.transpose(kernel_two, (1, 0, 2))
    vmem = pl.BlockSpec(memory_space=pltpu.VMEM)
    out = pl.pallas_call(
        kernel,
        out_shape=jax.ShapeDtypeStruct((2, 320, 128), BF),
        in_specs=[pl.BlockSpec(memory_space=pl.ANY)] + [vmem] * 13,
        out_specs=vmem,
        scratch_shapes=[
            pltpu.VMEM((2, 2, 320, 128), BF),
            pltpu.VMEM((4, 2, 16, 256), BF),
            pltpu.VMEM((8, 2, 16, 256), BF),
            pltpu.VMEM((2, 64, SLOT, 128), BF),
            pltpu.VMEM((6, 128, 1024), BF),
            pltpu.VMEM((4, 128, 320), F32),
            pltpu.VMEM((320, 1024), BF),
            pltpu.VMEM((384, 384), F32),
            pltpu.SemaphoreType.DMA, pltpu.SemaphoreType.DMA,
            pltpu.SemaphoreType.DMA((7,)), pltpu.SemaphoreType.DMA((7,)),
            pltpu.SemaphoreType.DMA((7,)), pltpu.SemaphoreType.DMA((7,)),
            pltpu.SemaphoreType.DMA((3, 8)), pltpu.SemaphoreType.DMA((3, 8)),
            pltpu.SemaphoreType.DMA((2,)), pltpu.SemaphoreType.DMA((2,)),
            pltpu.SemaphoreType.DMA, pltpu.SemaphoreType.DMA,
            pltpu.SemaphoreType.DMA,
        ],
        compiler_params=pltpu.CompilerParams(
            collective_id=0, has_side_effects=True, vmem_limit_bytes=40 * 2**20),
        name="residual_block",
    )(lat, mean_one, rstd_one, gain_one, shift_one, k1, bias_one, embed_bias,
      mean_two, rstd_two, gain_two, shift_two, k2, bias_two)
    return jnp.transpose(out, (0, 2, 1))[None]


def solution(mesh):
    placed = (
        P("dp", "rows", None, None), P("dp", None), P("dp", None), P(), P(), P(None, None, "dp"), P(),
        P("dp", None), P("dp", None), P("dp", None), P(), P(), P(None, None, "dp"), P(),
    )
    return jax.shard_map(
        shards, mesh=mesh, in_specs=placed, out_specs=P("dp", "rows", None, None), check_vma=False
    )
```

time: 1820 us -> 66.2 us (0.04)
  blocking collectives: 1590 us -> 0 us
  local copies, waits for them, and re-layouts: 201 us -> 9.08 us
  Pallas kernels: 0 us -> 56.7 us
    all_gather x8 -> x0, blocking collectives: 1590 us -> none  [convolve_blocks(): gathered = lax.all_gather(kernel[number], 'dp', axis=1, tiled=True)]
    all_gather x8 -> x0, local copies, waits for them, and re-layouts: 189 us -> none  [convolve_blocks(): gathered = lax.all_gather(kernel[number], 'dp', axis=1, tiled=True)]
    pallas_call x0 -> x1, Pallas kernels: none -> 56.7 us  [shards(): pl.pallas_call(kernel, out_shape=jax.ShapeDtypeStruct((2, 320, 128), BF),...]
  transfers between devices with their start and end apart: 4 -> 0, of which waited for: 0 -> 0; matrix products, arithmetic and copies ran while one was open for 11% -> 0% of each run, Pallas kernels for 0% -> 0%
where the time goes in v1:
time: 66.2 us; the launch traced here: 65.8 us
  Pallas kernels  56.7 us (86%)
  local copies, waits for them, and re-layouts  9.08 us (14%)
    pallas_call x1, Pallas kernels, shards(): pl.pallas_call(kernel, out_shape=jax.ShapeDtypeStruct((2, 320, 128), BF),...  56.7 us
    unnamed x29, local copies, waits for them, and re-layouts  9.08 us

profile of v1, /device:TPU:1, one launch (start us, length us, event | category | flops | bytes accessed | tf_op | source)
XLA Modules:
  0.0 65.8 jit_solution(138552021682375569)
XLA Ops:
  0.0 0.0 copy-start.4
  0.0 0.0 copy-start.3
  0.0 0.0 copy-start.9
  0.0 0.7 %copy-done.4 = f32[320]{0:T(512)S(1)} copy-done((f32[320]{0:T(512)S(1)}, f32[320]{0:T(512)}, u32[]{:S(2)}) %copy-start.4) | copy-done | bytes 1304
  0.7 0.0 copy-done.3
  0.7 0.0 copy-done.9
  0.7 0.0 copy-start
  0.7 0.9 %copy-done = bf16[1,2,128,320]{2,3,1,0:T(8,128)(2,1)S(1)} copy-done((bf16[1,2,128,320]{2,3,1,0:T(8,128)(2,1)S(1)}, bf16[1,2,128,320]{2,3,1,0:T(8,128)(2,1)}, u32[]{:S(2)}) %copy-start) | copy-done | bytes 163864
  1.6 0.0 copy-start.1
  1.6 0.7 %copy-done.1 = bf16[4,9,200]{2,0,1:T(4,128)(2,1)S(1)} copy-done((bf16[4,9,200]{2,0,1:T(4,128)(2,1)S(1)}, bf16[4,9,200]{2,0,1:T(4,128)(2,1)}, u32[]{:S(2)}) %copy-start.1) | copy-done | bytes 14424
  2.4 0.0 copy-start.2
  2.4 0.7 %copy-done.2 = bf16[4,9,200]{2,0,1:T(4,128)(2,1)S(1)} copy-done((bf16[4,9,200]{2,0,1:T(4,128)(2,1)S(1)}, bf16[4,9,200]{2,0,1:T(4,128)(2,1)}, u32[]{:S(2)}) %copy-start.2) | copy-done | bytes 14424
  3.1 0.0 copy-start.5
  3.1 0.7 %copy-done.5 = f32[320]{0:T(512)S(1)} copy-done((f32[320]{0:T(512)S(1)}, f32[320]{0:T(512)}, u32[]{:S(2)}) %copy-start.5) | copy-done | bytes 1304
  3.8 0.0 copy-start.6
  3.8 0.7 %copy-done.6 = f32[320]{0:T(512)S(1)} copy-done((f32[320]{0:T(512)S(1)}, f32[320]{0:T(512)}, u32[]{:S(2)}) %copy-start.6) | copy-done | bytes 1304
  4.4 0.0 copy-start.7
  4.4 0.7 %copy-done.7 = f32[320]{0:T(512)S(1)} copy-done((f32[320]{0:T(512)S(1)}, f32[320]{0:T(512)}, u32[]{:S(2)}) %copy-start.7) | copy-done | bytes 1304
  5.1 0.0 copy-start.8
  5.1 0.7 %copy-done.8 = f32[320]{0:T(512)S(1)} copy-done((f32[320]{0:T(512)S(1)}, f32[320]{0:T(512)}, u32[]{:S(2)}) %copy-start.8) | copy-done | bytes 1304
  5.8 0.0 copy-start.10
  5.8 0.7 copy-done.10
  6.5 0.0 copy-start.11
  6.5 0.7 copy-done.11
  7.1 0.0 copy-start.12
  7.1 0.7 copy-done.12
  7.8 0.0 copy-start.13
  7.8 0.7 copy-done.13
  8.4 56.7 %residual_block.1 = bf16[2,320,128]{2,1,0:T(8,128)(2,1)S(1)} custom-call(bf16[2,320,128]{2,1,0:T(8,128)(2,1)S(1)} %bitcast.9, f32[1,32]{1,0:T(1,128)S(1)} %copy-done.10, f32[1,32]{1,0:T(1,128)S(1)} %copy-done.11, f32[320]{0:T(512)S(1)} %copy-done.3, f32[320]{0:T(512)S(1)} %copy-done.4, bf16[9,4,200]{2,1,0:T(4,128)(2,1)S(1)} %bitcast.10, f32[320]{0:T(512)S(1)} %copy-done.5, ...), custom_call_target="tpu_custom_call" | custom-call | tf_op jit(solution)/shard_map/residual_block/pallas_call | solution.py:225
  65.1 0.7 %copy.16 = bf16[1,2,128,320]{2,3,1,0:T(8,128)(2,1)} copy(bf16[1,2,128,320]{2,3,1,0:T(8,128)(2,1)S(1)} %bitcast.8) | data formatting | bytes 327680
Async XLA Ops:
  0.0 0.7 %copy-start.4 = (f32[320]{0:T(512)S(1)}, f32[320]{0:T(512)}, u32[]{:S(2)}) copy-start(f32[320]{0:T(512)} %shift1.1) | copy-start | bytes 3844
  0.0 0.7 %copy-start.3 = (f32[320]{0:T(512)S(1)}, f32[320]{0:T(512)}, u32[]{:S(2)}) copy-start(f32[320]{0:T(512)} %gain1.1) | copy-start | bytes 3844
  0.0 0.7 %copy-start.9 = (f32[1,320]{1,0:T(1,128)S(1)}, f32[1,320]{1,0:T(1,128)}, u32[]{:S(2)}) copy-start(f32[1,320]{1,0:T(1,128)} %embed.1) | copy-start | bytes 3844
  0.7 0.9 %copy-start = (bf16[1,2,128,320]{2,3,1,0:T(8,128)(2,1)S(1)}, bf16[1,2,128,320]{2,3,1,0:T(8,128)(2,1)}, u32[]{:S(2)}) copy-start(bf16[1,2,128,320]{2,3,1,0:T(8,128)(2,1)} %param.14) | copy-start | bytes 491524
  1.6 0.7 %copy-start.1 = (bf16[4,9,200]{2,0,1:T(4,128)(2,1)S(1)}, bf16[4,9,200]{2,0,1:T(4,128)(2,1)}, u32[]{:S(2)}) copy-start(bf16[4,9,200]{2,0,1:T(4,128)(2,1)} %param.19) | copy-start | bytes 43204
  2.4 0.7 %copy-start.2 = (bf16[4,9,200]{2,0,1:T(4,128)(2,1)S(1)}, bf16[4,9,200]{2,0,1:T(4,128)(2,1)}, u32[]{:S(2)}) copy-start(bf16[4,9,200]{2,0,1:T(4,128)(2,1)} %param.26) | copy-start | bytes 43204
  3.1 0.7 %copy-start.5 = (f32[320]{0:T(512)S(1)}, f32[320]{0:T(512)}, u32[]{:S(2)}) copy-start(f32[320]{0:T(512)} %bias1.1) | copy-start | bytes 3844
  3.8 0.7 %copy-start.6 = (f32[320]{0:T(512)S(1)}, f32[320]{0:T(512)}, u32[]{:S(2)}) copy-start(f32[320]{0:T(512)} %gain2.1) | copy-start | bytes 3844
  4.4 0.7 %copy-start.7 = (f32[320]{0:T(512)S(1)}, f32[320]{0:T(512)}, u32[]{:S(2)}) copy-start(f32[320]{0:T(512)} %shift2.1) | copy-start | bytes 3844
  5.1 0.7 %copy-start.8 = (f32[320]{0:T(512)S(1)}, f32[320]{0:T(512)}, u32[]{:S(2)}) copy-start(f32[320]{0:T(512)} %bias2.1) | copy-start | bytes 3844
  5.8 0.7 copy-start.10
  6.5 0.7 copy-start.11
  7.1 0.7 copy-start.12
  7.8 0.7 copy-start.13

commit v2 on v1

v2 whole, which is shorter than its diff:
```python
from functools import partial

import jax
import jax.numpy as jnp
from jax import lax
from jax.experimental import pallas as pl
from jax.experimental.pallas import tpu as pltpu
from jax.sharding import PartitionSpec as P

MESH = pl.DeviceIdType.MESH
BF = jnp.bfloat16
F32 = jnp.float32
REL = (0, 1, -1, 2, -2, 3, -3, 4)
CHUNKS_A = ((0, 1), (1, 3), (3, 5), (5, 8))
CHUNKS_B = ((0, 5), (5, 8))
PART_A = (0, 96)
PART_B = (96, 128)
COPIES = 160
SWAPS = tuple((a, b) for a in range(4) for b in range(2) if (a, b) != (0, 0))
SLOT = 128


def device(x, y, z, c):
    x, y, z, c = x % 4, y % 4, z % 8, c % 2
    return ((((x % 2) * 8 + z) * 4 + y) * 2 + c, x // 2)


def silu_norm(values, mean, rstd, gain, shift):
    scaled = ((values - mean) * rstd) * gain + shift
    return scaled / (1.0 + jnp.exp(-scaled))


def spread(channel_values):
    group = lax.broadcasted_iota(jnp.int32, (32, 320), 0)
    lane = lax.broadcasted_iota(jnp.int32, (32, 320), 1)
    pick = jnp.where(lane // 10 == group, 1.0, 0.0).astype(F32)
    wide = jnp.broadcast_to(channel_values, (8, 32))
    return jnp.dot(wide, pick, precision=lax.Precision.HIGHEST, preferred_element_type=F32)[0:1]


def expand(act, pick, tap_lane):
    wide = jnp.dot(act, pick, preferred_element_type=F32)
    row = lax.broadcasted_iota(jnp.int32, (128, 1024), 0)
    before = jnp.where(row == 0, 0.0, pltpu.roll(wide, 1, 0))
    after = jnp.where(row == 127, 0.0, pltpu.roll(wide, 127, 0))
    return jnp.where(tap_lane < 5, before, jnp.where(tap_lane < 10, wide, after)).astype(BF)


def distance(place):
    return ((place + 1) // 2) * (2 * (place % 2) - 1)


def kernel(
    lat_ref, mean1, rstd1, gain1, shift1, k1_ref, bias1, embed, mean2, rstd2, gain2, shift2, k2_ref, bias2,
    out_ref,
    lat, raw, vectors, stats, msg, got, held, lhs, sample, pick, acc,
    lat_send, lat_recv, swap_send, swap_recv, sent, landed, local_sem,
):
    d = lax.axis_index("dp")
    h = lax.axis_index("rows")
    c = d % 2
    y = (d // 2) % 4
    z = (d // 8) % 8
    xl = d // 64
    x = 2 * h + xl

    local = []
    for i, (source, target) in enumerate((
        (k1_ref, raw.at[0]), (k2_ref, raw.at[1]), (lat_ref, lat.at[h]),
        (mean1, stats.at[0]), (rstd1, stats.at[1]), (mean2, stats.at[2]), (rstd2, stats.at[3]),
        (gain1, vectors.at[0]), (shift1, vectors.at[1]), (bias1, vectors.at[2]),
        (gain2, vectors.at[3]), (shift2, vectors.at[4]), (bias2, vectors.at[5]), (embed, vectors.at[pl.ds(6, 1)]),
    )):
        copy = pltpu.make_async_copy(source, target, local_sem.at[i])
        copy.start()
        local.append(copy)

    barrier = pltpu.get_barrier_semaphore()
    partners = [device(x, y - a, z, c - b) for a, b in SWAPS]
    partners += [device(x, y, z - s, c) for s in REL[1:]]
    partners += [device(x + s, y, z, c) for s in (1, 2, 3)]
    for partner in partners:
        pl.semaphore_signal(barrier, inc=1, device_id=partner, device_id_type=MESH)

    with jax.named_scope("messages"):
        msg[...] = jnp.zeros_like(msg)
        for number in range(2):
            local[number].wait()
            block = raw[number].astype(F32)
            for b in range(4):
                msg[b, number, 0:9, 0:200] = block[:, b, :].astype(BF)

    with jax.named_scope("barrier"):
        pl.semaphore_wait(barrier, len(partners))

    swaps = []
    q = 2 * y + c
    for i, (a, b) in enumerate(SWAPS):
        to_y = (y + a) % 4
        copy = pltpu.make_async_remote_copy(
            src_ref=msg.at[to_y], dst_ref=got.at[q], send_sem=swap_send.at[i], recv_sem=swap_recv.at[i],
            device_id=device(x, y + a, z, c + b), device_id_type=MESH)
        copy.start()
        swaps.append(copy)
    lat_copy = pltpu.make_async_remote_copy(
        src_ref=lat_ref, dst_ref=lat.at[h], send_sem=lat_send, recv_sem=lat_recv,
        device_id=device(x + 2, y, z, c), device_id_type=MESH)
    lat_copy.start()
    got[q] = msg[y]

    with jax.named_scope("pick"):
        lane = lax.broadcasted_iota(jnp.int32, (1, 1024), 1)
        within = lane % 16
        group = lane // 16
        zz = (z + distance(group % 8) + 8) % 8
        bb = (y + distance((group // 8) % 4) + 4) % 4
        xx = (xl + group // 32) % 2
        wanted = jnp.where(within < 15, bb * 80 + (xx * 8 + zz) * 5 + within % 5, -1)
        channel = lax.broadcasted_iota(jnp.int32, (320, 1024), 0)
        pick[...] = jnp.where(wanted == channel, 1.0, 0.0).astype(BF)

    with jax.named_scope("swap"):
        for copy in swaps:
            copy.wait_recv()

    with jax.named_scope("assemble"):
        col = lax.broadcasted_iota(jnp.int32, (16, 384), 1)
        row48 = lax.broadcasted_iota(jnp.int32, (48, 80), 0)
        col80 = lax.broadcasted_iota(jnp.int32, (48, 80), 1)
        in_tile = row48 % 16
        source = (in_tile % 5) * 16 + (row48 // 16) * 3 + in_tile // 5
        place = jnp.where((source == col80) & (in_tile < 15), 1.0, 0.0).astype(BF)
        whole = []
        for number in range(2):
            pieces = [
                jnp.concatenate([got[i, number].astype(F32), jnp.zeros((16, 128), F32)], axis=1) for i in range(8)
            ]
            rows = []
            for p in range(5):
                total = jnp.zeros((16, 384), F32)
                for i in range(8):
                    by = 200 * i - 320 * p
                    low, high = max(0, -by), min(200, 320 - by)
                    if low < high:
                        part = jnp.where((col >= low) & (col < high), pieces[i], 0.0)
                        total = total + (pltpu.roll(part, by % 384, 1) if by % 384 else part)
                rows.append(total)
            stacked = jnp.concatenate(rows, axis=0).astype(BF)
            whole.append(jnp.dot(place, stacked, preferred_element_type=F32))
        one, two = whole
        first = c == 0
        own = held.at[0, 0, 0, 0]
        own[0:48] = jnp.where(first, one[:, 0:128], one[:, 128:256]).astype(BF)
        own[80:128] = jnp.where(first, two[:, 0:128], two[:, 128:256]).astype(BF)
        last = one[:, 256:384] + pltpu.roll(two[:, 256:384], 64, 1)
        own[48:80] = jnp.where(first, last[0:32], last[16:48]).astype(BF)

    copies = []
    count = [0]

    def send(source, target, to, recv=None):
        i = len(copies)
        if recv is None:
            recv = landed.at[count[0]]
            count[0] += 1
        copy = pltpu.make_async_remote_copy(
            src_ref=source, dst_ref=target, send_sem=sent.at[i], recv_sem=recv, device_id=to, device_id_type=MESH)
        copy.start()
        copies.append(copy)
        return copy

    class Part:
        def __init__(self, span, chunks):
            self.low, self.high = span
            self.size = self.high - self.low
            self.half = pl.ds(self.low + h * (self.size // 2), self.size // 2)
            self.chunks = chunks
            self.z, self.y, self.yy, self.x, self.c = {}, {}, {}, {}, []

        def at(self, xr, yr, chunk, core=0):
            ys = yr if isinstance(yr, int) else pl.ds(yr[0], yr[1] - yr[0])
            low, high = chunk
            return held.at[core, xr, ys, pl.ds(low, high - low), pl.ds(self.low, self.size)]

        def half_at(self, xr, yr, chunk):
            low, high = chunk
            return held.at[0, xr, pl.ds(yr[0], yr[1] - yr[0]), pl.ds(low, high - low), self.half]

        def send_z(self):
            for i in range(1, 8):
                back = REL.index(-REL[i]) if REL[i] != 4 else 7
                self.z[back] = send(self.at(0, 0, (0, 1)), self.at(0, 0, (back, back + 1)), device(x, y, z + REL[i], c))

        def send_y(self, k):
            chunk = self.chunks[k]
            up = send(self.at(0, 0, chunk), self.at(0, 2, chunk), device(x, y + 1, z, c))
            down = send(self.at(0, 0, chunk), self.at(0, 1, chunk), device(x, y - 1, z, c))
            self.y[k] = (up, down)

        def send_x(self, k, ys):
            chunk = self.chunks[k]
            base = count[0]
            count[0] += 2
            for s in (1, -1):
                copy = send(self.half_at(0, ys, chunk), self.half_at(1, ys, chunk), device(x + s, y, z, c),
                            landed.at[base + h])
            self.x.setdefault(k, []).append((base, copy, ys))

        def wait_x(self, k):
            for base, copy, ys in self.x[k]:
                for side in range(2):
                    ref = self.half_at(1, ys, self.chunks[k])
                    pltpu.make_async_remote_copy(
                        src_ref=ref, dst_ref=ref, send_sem=sent.at[0], recv_sem=landed.at[base + side],
                        device_id=device(x + 1, y, z, c), device_id_type=MESH).wait_recv()

        def send_c(self, k, xr):
            chunk = self.chunks[k]
            self.c.append(send(self.at(xr, (0, 4), chunk), self.at(xr, (0, 4), chunk, 1), device(x, y, z, c + 1)))

        def after_z(self, k):
            for i in range(*self.chunks[k]):
                if i:
                    self.z[i].wait_recv()
            self.send_y(k)
            self.send_x(k, (0, 1))

        def after_y(self, k):
            for copy in self.y[k]:
                copy.wait_recv()
            chunk = self.chunks[k]
            if k in (0, 3) or (len(self.chunks) == 2 and k == 1):
                self.yy[k] = send(self.at(0, 2, chunk), self.at(0, 3, chunk), device(x, y + 1, z, c))
            else:
                self.yy[k] = send(self.at(0, 1, chunk), self.at(0, 3, chunk), device(x, y - 1, z, c))
            self.send_x(k, (1, 3))

        def after_yy(self, k):
            self.yy[k].wait_recv()
            self.send_x(k, (3, 4))
            self.send_c(k, 0)

        def after_x(self, k):
            self.wait_x(k)
            self.send_c(k, 1)

    a, b = Part(PART_A, CHUNKS_A), Part(PART_B, CHUNKS_B)
    with jax.named_scope("send_first"):
        a.send_z()
        a.after_z(0)
        b.send_z()

    tap_lane = lax.broadcasted_iota(jnp.int32, (128, 1024), 1) % 16

    def vector(i):
        return vectors[i : i + 1]

    with jax.named_scope("gather_1"):
        a.after_z(1)
        a.after_y(0)
        a.after_z(2)
    with jax.named_scope("stats"):
        for copy in local[2:]:
            copy.wait()
        lat_copy.wait_recv()
        m1, r1 = spread(stats[0]), spread(stats[1])
        m2, r2 = spread(stats[2]), spread(stats[3])
        lhs[0] = jnp.zeros((128, 1024), BF)
        lhs[5] = jnp.zeros((128, 1024), BF)

    def activate(r):
        with jax.named_scope("activate"):
            values = lat[r // 2, r % 2].astype(F32).T
            sample[r] = values
            lhs[r + 1] = expand(silu_norm(values, m1, r1, vector(0), vector(1)).astype(BF), pick[...], tap_lane)

    with jax.named_scope("gather_2"):
        a.after_y(1)
        a.after_z(3)
    activate(0)
    with jax.named_scope("gather_3"):
        a.after_yy(0)
        a.after_y(2)
        b.after_z(0)
    activate(1)
    with jax.named_scope("gather_4"):
        a.after_yy(1)
        a.after_y(3)
        b.after_z(1)
    activate(2)
    with jax.named_scope("gather_5"):
        a.after_yy(2)
        b.after_y(0)
        a.after_x(0)
        a.after_yy(3)
        b.after_y(1)
    activate(3)
    with jax.named_scope("gather_6"):
        a.after_x(1)
        b.after_yy(0)
        a.after_x(2)
        b.after_yy(1)
        a.after_x(3)
    with jax.named_scope("sibling_a"):
        for copy in a.c:
            copy.wait_recv()

    def weights(dy, base):
        t0 = held[c, :, :, :, base + 16 * dy : base + 16 * dy + 16].reshape(1024, 128)
        t1 = held[1 - c, :, :, :, base + 16 * dy : base + 16 * dy + 16].reshape(1024, 128)
        owner, at = ((c, 48), (c, 64), (1 - c, 64))[dy]
        t2 = held[owner, :, :, :, at : at + 16].reshape(1024, 128)
        return jnp.concatenate([t0, t1, t2], axis=1)

    with jax.named_scope("conv_one"):
        for dy in range(3):
            left = lhs[pl.ds(h + dy, 3)].reshape(384, 1024)
            product = jnp.dot(left, weights(dy, 0), preferred_element_type=F32)
            if dy:
                acc[...] += product
            else:
                acc[...] = product

    with jax.named_scope("gather_b"):
        for k in range(len(CHUNKS_B)):
            b.after_x(k)

    with jax.named_scope("second_activation"):
        offset = vector(2) + vector(6)
        for r in range(3):
            hidden = acc[128 * r : 128 * r + 128, 0:320] + offset
            lhs[r + 1] = expand(silu_norm(hidden, m2, r2, vector(3), vector(4)).astype(BF), pick[...], tap_lane)
        lhs[4] = jnp.zeros((128, 1024), BF)
    with jax.named_scope("sibling_b"):
        for copy in b.c:
            copy.wait_recv()
    with jax.named_scope("conv_two"):
        for dy in range(3):
            left = lhs[pl.ds(h + dy, 2)].reshape(256, 1024)
            product = jnp.dot(left, weights(dy, 80), preferred_element_type=F32)
            if dy:
                acc[0:256] += product
            else:
                acc[0:256] = product
    with jax.named_scope("result"):
        for r in range(2):
            rows = acc[128 * r : 128 * r + 128]
            result = jnp.concatenate([rows[:, 0:256], rows[:, 320:384]], axis=1)
            out_ref[r] = ((result + vector(5) + sample[2 * h + r]).T).astype(BF)
    with jax.named_scope("sends"):
        for copy in swaps + [lat_copy] + copies:
            copy.wait_send()


def shards(latents, mean_one, rstd_one, gain_one, shift_one, kernel_one, bias_one, embed_bias,
           mean_two, rstd_two, gain_two, shift_two, kernel_two, bias_two):
    lat = jnp.transpose(latents[0], (0, 2, 1))
    k1 = jnp.transpose(kernel_one, (1, 0, 2))
    k2 = jnp.transpose(kernel_two, (1, 0, 2))
    vmem = pl.BlockSpec(memory_space=pltpu.VMEM)
    out = pl.pallas_call(
        kernel,
        out_shape=jax.ShapeDtypeStruct((2, 320, 128), BF),
        in_specs=[pl.BlockSpec(memory_space=pltpu.HBM)] * 14,
        out_specs=vmem,
        scratch_shapes=[
            pltpu.VMEM((2, 2, 320, 128), BF),
            pltpu.VMEM((2, 9, 4, 200), BF),
            pltpu.VMEM((8, 320), F32),
            pltpu.VMEM((4, 1, 32), F32),
            pltpu.VMEM((4, 2, 16, 256), BF),
            pltpu.VMEM((8, 2, 16, 256), BF),
            pltpu.VMEM((2, 2, 4, 8, SLOT, 128), BF),
            pltpu.VMEM((6, 128, 1024), BF),
            pltpu.VMEM((4, 128, 320), F32),
            pltpu.VMEM((320, 1024), BF),
            pltpu.VMEM((384, 384), F32),
            pltpu.SemaphoreType.DMA, pltpu.SemaphoreType.DMA,
            pltpu.SemaphoreType.DMA((7,)), pltpu.SemaphoreType.DMA((7,)),
            pltpu.SemaphoreType.DMA((COPIES,)), pltpu.SemaphoreType.DMA((COPIES,)),
            pltpu.SemaphoreType.DMA((14,)),
        ],
        compiler_params=pltpu.CompilerParams(
            collective_id=0, has_side_effects=True, vmem_limit_bytes=60 * 2**20),
        name="residual_block",
    )(lat, mean_one, rstd_one, gain_one, shift_one, k1, bias_one, embed_bias,
      mean_two, rstd_two, gain_two, shift_two, k2, bias_two)
    return jnp.transpose(out, (0, 2, 1))[None]


def solution(mesh):
    placed = (
        P("dp", "rows", None, None), P("dp", None), P("dp", None), P(), P(), P(None, None, "dp"), P(),
        P("dp", None), P("dp", None), P("dp", None), P(), P(), P(None, None, "dp"), P(),
    )
    return jax.shard_map(
        shards, mesh=mesh, in_specs=placed, out_specs=P("dp", "rows", None, None), check_vma=False
    )
```

time: 66.2 us -> 45.6 us (0.69)
  Pallas kernels: 56.7 us -> 43.9 us
  local copies, waits for them, and re-layouts: 9.08 us -> 1.59 us
    pallas_call x1, Pallas kernels: 56.7 us -> 43.9 us  [shards(): pl.pallas_call(kernel, out_shape=jax.ShapeDtypeStruct((2, 320, 128), BF),...]
    unnamed x29 -> x1, local copies, waits for them, and re-layouts: 9.08 us -> 1.59 us
where the time goes in v2:
time: 45.6 us; the launch traced here: 45.5 us
  Pallas kernels  43.9 us (96%)
  local copies, waits for them, and re-layouts  1.59 us (3%)
    pallas_call x1, Pallas kernels, shards(): pl.pallas_call(kernel, out_shape=jax.ShapeDtypeStruct((2, 320, 128), BF),...  43.9 us
    unnamed x1, local copies, waits for them, and re-layouts  1.59 us

profile of v2, /device:TPU:1, one launch (start us, length us, event | category | flops | bytes accessed | tf_op | source)
XLA Modules:
  0.0 45.5 jit_solution(11699651684669345802)
XLA Ops:
  0.0 43.9 %residual_block.1 = bf16[2,320,128]{2,1,0:T(8,128)(2,1)} custom-call(bf16[2,320,128]{2,1,0:T(8,128)(2,1)} %bitcast.9, f32[1,32]{1,0:T(1,128)} %mean1.1, f32[1,32]{1,0:T(1,128)} %rstd1.1, f32[320]{0:T(512)} %gain1.1, f32[320]{0:T(512)} %shift1.1, bf16[9,4,200]{2,1,0:T(4,128)(2,1)} %bitcast.10, f32[320]{0:T(512)} %bias1.1, f32[1,320]{1,0:T(1,128)} %embed.1, ...), custom_call_target="tpu_custom_call" | custom-call | tf_op jit(solution)/shard_map/residual_block/pallas_call | solution.py:361
  43.9 1.6 %copy.16 = bf16[1,2,128,320]{2,3,1,0:T(8,128)(2,1)} copy(bf16[1,2,128,320]{2,3,1,0:T(8,128)(2,1)} %bitcast.8) | data formatting | bytes 327680

commit v3 on v1

v3 whole, which is shorter than its diff:
```python
from functools import partial

import jax
import jax.numpy as jnp
from jax import lax
from jax.experimental import pallas as pl
from jax.experimental.pallas import tpu as pltpu
from jax.sharding import PartitionSpec as P

MESH = pl.DeviceIdType.MESH
BF = jnp.bfloat16
F32 = jnp.float32
REL = (0, 1, -1, 2, -2, 3, -3, 4)
CHUNKS = ((0, 1), (1, 3), (3, 5), (5, 7), (7, 8))
Z_ORDER = (1, 2, 3, 4, 5, 6, 7)
FAR = ()
COPIES = 64
SWAPS = tuple((a, b) for a in range(4) for b in range(2) if (a, b) != (0, 0))
SLOT = 128


def device(x, y, z, c):
    x, y, z, c = x % 4, y % 4, z % 8, c % 2
    return ((((x % 2) * 8 + z) * 4 + y) * 2 + c, x // 2)


def silu_norm(values, mean, rstd, gain, shift):
    scaled = ((values - mean) * rstd) * gain + shift
    return scaled / (1.0 + jnp.exp(-scaled))


def spread(channel_values):
    group = lax.broadcasted_iota(jnp.int32, (32, 320), 0)
    lane = lax.broadcasted_iota(jnp.int32, (32, 320), 1)
    pick = jnp.where(lane // 10 == group, 1.0, 0.0).astype(F32)
    wide = jnp.broadcast_to(channel_values, (8, 32))
    return jnp.dot(wide, pick, precision=lax.Precision.HIGHEST, preferred_element_type=F32)[0:1]


def expand(act, pick, tap_lane):
    wide = jnp.dot(act, pick, preferred_element_type=F32)
    row = lax.broadcasted_iota(jnp.int32, (128, 1024), 0)
    before = jnp.where(row == 0, 0.0, pltpu.roll(wide, 1, 0))
    after = jnp.where(row == 127, 0.0, pltpu.roll(wide, 127, 0))
    return jnp.where(tap_lane < 5, before, jnp.where(tap_lane < 10, wide, after)).astype(BF)


def distance(place):
    return ((place + 1) // 2) * (2 * (place % 2) - 1)


def kernel(
    lat_ref, mean1, rstd1, gain1, shift1, k1_ref, bias1, embed, mean2, rstd2, gain2, shift2, k2_ref, bias2,
    out_ref,
    lat, raw, vectors, stats, msg, got, held, lhs, sample, pick, acc,
    lat_send, lat_recv, swap_send, swap_recv, sent, landed, local_sem,
):
    d = lax.axis_index("dp")
    h = lax.axis_index("rows")
    c = d % 2
    y = (d // 2) % 4
    z = (d // 8) % 8
    xl = d // 64
    x = 2 * h + xl

    local = []
    for i, (source, target) in enumerate((
        (k1_ref, raw.at[0]), (k2_ref, raw.at[1]), (lat_ref, lat.at[h]),
        (mean1, stats.at[0]), (rstd1, stats.at[1]), (mean2, stats.at[2]), (rstd2, stats.at[3]),
        (gain1, vectors.at[0]), (shift1, vectors.at[1]), (bias1, vectors.at[2]),
        (gain2, vectors.at[3]), (shift2, vectors.at[4]), (bias2, vectors.at[5]), (embed, vectors.at[pl.ds(6, 1)]),
    )):
        copy = pltpu.make_async_copy(source, target, local_sem.at[i])
        copy.start()
        local.append(copy)

    barrier = pltpu.get_barrier_semaphore()
    partners = [device(x, y - a, z, c - b) for a, b in SWAPS]
    partners += [device(x, y, z - s, c) for s in REL[1:]]
    partners += [device(x + s, y, z, c) for s in (1, 2, 3)]
    for partner in partners:
        pl.semaphore_signal(barrier, inc=1, device_id=partner, device_id_type=MESH)

    msg[...] = jnp.zeros_like(msg)
    for number in range(2):
        local[number].wait()
        block = raw[number].astype(F32)
        for b in range(4):
            msg[b, number, 0:9, 0:200] = block[:, b, :].astype(BF)

    pl.semaphore_wait(barrier, len(partners))

    swaps = []
    q = 2 * y + c
    for i, (a, b) in enumerate(SWAPS):
        copy = pltpu.make_async_remote_copy(
            src_ref=msg.at[(y + a + 2 * h) % 4], dst_ref=got.at[q], send_sem=swap_send.at[i], recv_sem=swap_recv.at[i],
            device_id=device(x, y + a, z, c + b), device_id_type=MESH)
        copy.start()
        swaps.append(copy)
    lat_copy = pltpu.make_async_remote_copy(
        src_ref=lat_ref, dst_ref=lat.at[h], send_sem=lat_send, recv_sem=lat_recv,
        device_id=device(x + 2, y, z, c), device_id_type=MESH)
    lat_copy.start()
    got[q] = msg[(y + 2 * h) % 4]

    lane = lax.broadcasted_iota(jnp.int32, (1, 1024), 1)
    within = lane % 16
    group = lane // 16
    zz = (z + distance(group % 8) + 8) % 8
    side = group // 32
    row = (group // 8) % 4
    bb = (y + jnp.where(side == 0, distance(row) + 2 * h, row) + 4) % 4
    xx = (xl + side) % 2
    wanted = jnp.where(within < 15, bb * 80 + (xx * 8 + zz) * 5 + within % 5, -1)
    channel = lax.broadcasted_iota(jnp.int32, (320, 1024), 0)
    pick[...] = jnp.where(wanted == channel, 1.0, 0.0).astype(BF)

    tap_lane = lax.broadcasted_iota(jnp.int32, (128, 1024), 1) % 16

    def vector(i):
        return vectors[i : i + 1]

    for copy in local[2:]:
        copy.wait()
    m1, r1 = spread(stats[0]), spread(stats[1])
    m2, r2 = spread(stats[2]), spread(stats[3])
    lhs[0] = jnp.zeros((128, 1024), BF)
    lhs[5] = jnp.zeros((128, 1024), BF)

    def activate(half, r):
        values = lat[half, r].astype(F32).T
        sample[2 * half + r] = values
        lhs[2 * half + r + 1] = expand(
            silu_norm(values, m1, r1, vector(0), vector(1)).astype(BF), pick[...], tap_lane)

    activate(h, 0)
    activate(h, 1)

    for copy in swaps:
        copy.wait_recv()

    col = lax.broadcasted_iota(jnp.int32, (16, 384), 1)
    row48 = lax.broadcasted_iota(jnp.int32, (48, 80), 0)
    col80 = lax.broadcasted_iota(jnp.int32, (48, 80), 1)
    in_tile = row48 % 16
    source = (in_tile % 5) * 16 + (row48 // 16) * 3 + in_tile // 5
    place = jnp.where((source == col80) & (in_tile < 15), 1.0, 0.0).astype(BF)
    whole = []
    for number in range(2):
        pieces = [
            jnp.concatenate([got[i, number].astype(F32), jnp.zeros((16, 128), F32)], axis=1) for i in range(8)
        ]
        rows = []
        for p in range(5):
            total = jnp.zeros((16, 384), F32)
            for i in range(8):
                by = 200 * i - 320 * p
                low, high = max(0, -by), min(200, 320 - by)
                if low < high:
                    part = jnp.where((col >= low) & (col < high), pieces[i], 0.0)
                    total = total + (pltpu.roll(part, by % 384, 1) if by % 384 else part)
            rows.append(total)
        stacked = jnp.concatenate(rows, axis=0).astype(BF)
        whole.append(jnp.dot(place, stacked, preferred_element_type=F32))
    one, two = whole
    first = c == 0
    own = held.at[0, 0, 0, 0]
    own[0:48] = jnp.where(first, one[:, 0:128], one[:, 128:256]).astype(BF)
    own[80:128] = jnp.where(first, two[:, 0:128], two[:, 128:256]).astype(BF)
    last = one[:, 256:384] + pltpu.roll(two[:, 256:384], 64, 1)
    own[48:80] = jnp.where(first, last[0:32], last[16:48]).astype(BF)

    up, down, far = device(x, y + 1, z, c), device(x, y - 1, z, c), device(x, y + 2, z, c)
    right, left, sibling = device(x + 1, y, z, c), device(x - 1, y, z, c), device(x, y, z, c + 1)
    copies = []
    count = [0]

    def send(source, target, to, recv=None):
        i = len(copies)
        if recv is None:
            recv = landed.at[count[0]]
            count[0] += 1
        copy = pltpu.make_async_remote_copy(
            src_ref=source, dst_ref=target, send_sem=sent.at[i], recv_sem=recv, device_id=to, device_id_type=MESH)
        copy.start()
        copies.append(copy)
        return copy

    def at(xr, yr, chunk, core=0):
        low, high = chunk
        return held.at[core, xr, yr, pl.ds(low, high - low)]

    z_copies, y_copies, far_copies, x_copies, core_copies = {}, {}, {}, {}, ({}, {})

    def send_z():
        for i in Z_ORDER:
            back = REL.index(-REL[i]) if REL[i] != 4 else 7
            z_copies[back] = send(at(0, 0, (0, 1)), at(0, 0, (back, back + 1)), device(x, y, z + REL[i], c))

    def send_x(k, j):
        base = count[0]
        count[0] += 2
        for to in (right, left):
            send(at(0, j, CHUNKS[k]), at(1, 2 * h + j, CHUNKS[k]), to, landed.at[base + h])
        x_copies.setdefault(k, []).append(base)

    def send_core(k, xr):
        ys = pl.ds(0, 4)
        core_copies[xr][k] = send(at(xr, ys, CHUNKS[k]), at(xr, ys, CHUNKS[k], 1), sibling)

    def after_z(k):
        chunk = CHUNKS[k]
        for i in range(*chunk):
            if i:
                z_copies[i].wait_recv()
        y_copies[k] = send(at(0, 0, chunk), at(0, 1, chunk), down), send(at(0, 0, chunk), at(0, 2, chunk), up)
        if k in FAR:
            far_copies[k] = send(at(0, 0, chunk), at(0, 3, chunk), far)
        send_x(k, 0)

    def after_y(k):
        chunk = CHUNKS[k]
        from_up, from_down = y_copies[k]
        from_up.wait_recv()
        if k % 2 and k not in FAR:
            far_copies[k] = send(at(0, 1, chunk), at(0, 3, chunk), down)
        send_x(k, 1)
        from_down.wait_recv()
        if k % 2 == 0 and k not in FAR:
            far_copies[k] = send(at(0, 2, chunk), at(0, 3, chunk), up)

    def after_far(k):
        far_copies[k].wait_recv()
        send_core(k, 0)

    def after_x(k):
        for base in x_copies[k]:
            for side in range(2):
                ref = at(1, 0, CHUNKS[k])
                pltpu.make_async_remote_copy(
                    src_ref=ref, dst_ref=ref, send_sem=sent.at[0], recv_sem=landed.at[base + side],
                    device_id=right, device_id_type=MESH).wait_recv()
        send_core(k, 1)

    send_z()
    after_z(0)
    lat_copy.wait_recv()
    activate(1 - h, 0)
    after_z(1)
    after_y(0)
    activate(1 - h, 1)
    after_z(2)
    after_y(1)
    after_z(3)
    after_far(0)
    after_z(4)
    after_y(2)
    after_far(1)
    after_y(3)
    after_y(4)
    after_far(2)
    after_x(0)
    after_x(1)
    after_far(3)
    after_far(4)
    after_x(2)
    after_x(3)
    after_x(4)

    def weights(dy, base, half):
        t0 = held[c, half, :, :, base + 16 * dy : base + 16 * dy + 16].reshape(512, 128)
        t1 = held[1 - c, half, :, :, base + 16 * dy : base + 16 * dy + 16].reshape(512, 128)
        owner, row = ((c, 48), (c, 64), (1 - c, 64))[dy]
        t2 = held[owner, half, :, :, row : row + 16].reshape(512, 128)
        return jnp.concatenate([t0, t1, t2], axis=1)

    def convolve(rows, base, half):
        for dy in range(3):
            left_side = lhs[pl.ds(h + dy, rows), :, 512 * half : 512 * half + 512].reshape(128 * rows, 512)
            product = jnp.dot(left_side, weights(dy, base, half), preferred_element_type=F32)
            if dy or half:
                acc[0 : 128 * rows] += product
            else:
                acc[0 : 128 * rows] = product

    for copy in core_copies[0].values():
        copy.wait_recv()
    convolve(3, 0, 0)
    for copy in core_copies[1].values():
        copy.wait_recv()
    convolve(3, 0, 1)

    offset = vector(2) + vector(6)
    for r in range(3):
        hidden = acc[128 * r : 128 * r + 128, 0:320] + offset
        lhs[r + 1] = expand(silu_norm(hidden, m2, r2, vector(3), vector(4)).astype(BF), pick[...], tap_lane)
    lhs[4] = jnp.zeros((128, 1024), BF)
    convolve(2, 80, 0)
    convolve(2, 80, 1)
    for r in range(2):
        rows = acc[128 * r : 128 * r + 128]
        result = jnp.concatenate([rows[:, 0:256], rows[:, 320:384]], axis=1)
        out_ref[r] = ((result + vector(5) + sample[2 * h + r]).T).astype(BF)
    for copy in swaps + [lat_copy] + copies:
        copy.wait_send()


def shards(latents, mean_one, rstd_one, gain_one, shift_one, kernel_one, bias_one, embed_bias,
           mean_two, rstd_two, gain_two, shift_two, kernel_two, bias_two):
    lat = jnp.transpose(latents[0], (0, 2, 1))
    k1 = jnp.transpose(kernel_one, (1, 0, 2))
    k2 = jnp.transpose(kernel_two, (1, 0, 2))
    vmem = pl.BlockSpec(memory_space=pltpu.VMEM)
    pin = lambda v: pltpu.with_memory_space_constraint(v, pltpu.HBM)
    out = pl.pallas_call(
        kernel,
        out_shape=jax.ShapeDtypeStruct((2, 320, 128), BF),
        in_specs=[pl.BlockSpec(memory_space=pltpu.HBM)] * 14,
        out_specs=vmem,
        scratch_shapes=[
            pltpu.VMEM((2, 2, 320, 128), BF),
            pltpu.VMEM((2, 9, 4, 200), BF),
            pltpu.VMEM((8, 320), F32),
            pltpu.VMEM((4, 1, 32), F32),
            pltpu.VMEM((4, 2, 16, 256), BF),
            pltpu.VMEM((8, 2, 16, 256), BF),
            pltpu.VMEM((2, 2, 4, 8, SLOT, 128), BF),
            pltpu.VMEM((6, 128, 1024), BF),
            pltpu.VMEM((4, 128, 320), F32),
            pltpu.VMEM((320, 1024), BF),
            pltpu.VMEM((384, 384), F32),
            pltpu.SemaphoreType.DMA, pltpu.SemaphoreType.DMA,
            pltpu.SemaphoreType.DMA((7,)), pltpu.SemaphoreType.DMA((7,)),
            pltpu.SemaphoreType.DMA((COPIES,)), pltpu.SemaphoreType.DMA((COPIES,)),
            pltpu.SemaphoreType.DMA((14,)),
        ],
        compiler_params=pltpu.CompilerParams(
            collective_id=0, has_side_effects=True, vmem_limit_bytes=40 * 2**20),
        name="residual_block",
    )(*map(pin, (lat, mean_one, rstd_one, gain_one, shift_one, k1, bias_one, embed_bias,
      mean_two, rstd_two, gain_two, shift_two, k2, bias_two)))
    return jnp.transpose(out, (0, 2, 1))[None]


def solution(mesh):
    placed = (
        P("dp", "rows", None, None), P("dp", None), P("dp", None), P(), P(), P(None, None, "dp"), P(),
        P("dp", None), P("dp", None), P("dp", None), P(), P(), P(None, None, "dp"), P(),
    )
    return jax.shard_map(
        shards, mesh=mesh, in_specs=placed, out_specs=P("dp", "rows", None, None), check_vma=False
    )
```

time: 66.2 us -> 38.2 us (0.58)
  Pallas kernels: 56.7 us -> 37.4 us
  local copies, waits for them, and re-layouts: 9.08 us -> 0.67 us
    pallas_call x1, Pallas kernels: 56.7 us -> 37.4 us  [shards(): pl.pallas_call(kernel, out_shape=jax.ShapeDtypeStruct((2, 320, 128), BF),...]
    unnamed x29 -> x1, local copies, waits for them, and re-layouts: 9.08 us -> 0.67 us
where the time goes in v3:
time: 38.2 us; the launch traced here: 38.1 us
  Pallas kernels  37.4 us (98%)
  local copies, waits for them, and re-layouts  0.67 us (2%)
    pallas_call x1, Pallas kernels, shards(): pl.pallas_call(kernel, out_shape=jax.ShapeDtypeStruct((2, 320, 128), BF),...  37.4 us

profile of v3, /device:TPU:1, one launch (start us, length us, event | category | flops | bytes accessed | tf_op | source)
XLA Modules:
  0.0 38.1 jit_solution(724854420112071472)
XLA Ops:
  0.0 37.4 %residual_block.1 = bf16[2,320,128]{2,1,0:T(8,128)(2,1)S(1)} custom-call(bf16[2,320,128]{2,1,0:T(8,128)(2,1)} %bitcast.9, f32[1,32]{1,0:T(1,128)} %mean1.1, f32[1,32]{1,0:T(1,128)} %rstd1.1, f32[320]{0:T(512)} %gain1.1, f32[320]{0:T(512)} %shift1.1, bf16[9,4,200]{2,1,0:T(4,128)(2,1)} %bitcast.10, f32[320]{0:T(512)} %bias1.1, f32[1,320]{1,0:T(1,128)} %embed.1, ...), custom_call_target="tpu_custom_call" | custom-call | tf_op jit(solution)/shard_map/residual_block/pallas_call | solution.py:316
  37.4 0.7 %copy.16 = bf16[1,2,128,320]{2,3,1,0:T(8,128)(2,1)} copy(bf16[1,2,128,320]{2,3,1,0:T(8,128)(2,1)S(1)} %bitcast.8) | data formatting | bytes 327680

commit v4 on v3

--- a/solution.py
+++ b/solution.py
@@ -11,7 +11,7 @@
 BF = jnp.bfloat16
 F32 = jnp.float32
 REL = (0, 1, -1, 2, -2, 3, -3, 4)
-CHUNKS = ((0, 1), (1, 3), (3, 5), (5, 7), (7, 8))
+CHUNKS = ((0, 1), (1, 3), (3, 5), (5, 8))
 Z_ORDER = (1, 2, 3, 4, 5, 6, 7)
 FAR = ()
 COPIES = 64
@@ -20,8 +20,8 @@
 
 
 def device(x, y, z, c):
-    x, y, z, c = x % 4, y % 4, z % 8, c % 2
-    return ((((x % 2) * 8 + z) * 4 + y) * 2 + c, x // 2)
+    x, y, z, c = lax.rem(x + 4, 4), lax.rem(y + 4, 4), lax.rem(z + 8, 8), lax.rem(c + 2, 2)
+    return (lax.rem(x, 2) * 64 + z * 8 + y * 2 + c, lax.div(x, 2))
 
 
 def silu_norm(values, mean, rstd, gain, shift):
@@ -63,6 +63,13 @@
     xl = d // 64
     x = 2 * h + xl
 
+    barrier = pltpu.get_barrier_semaphore()
+    partners = [device(x, y - a, z, c - b) for a, b in SWAPS]
+    partners += [device(x, y, z - s, c) for s in REL[1:]]
+    partners += [device(x + s, y, z, c) for s in (1, 2, 3)]
+    for partner in partners:
+        pl.semaphore_signal(barrier, inc=1, device_id=partner, device_id_type=MESH)
+
     local = []
     for i, (source, target) in enumerate((
         (k1_ref, raw.at[0]), (k2_ref, raw.at[1]), (lat_ref, lat.at[h]),
@@ -73,13 +80,6 @@
         copy = pltpu.make_async_copy(source, target, local_sem.at[i])
         copy.start()
         local.append(copy)
-
-    barrier = pltpu.get_barrier_semaphore()
-    partners = [device(x, y - a, z, c - b) for a, b in SWAPS]
-    partners += [device(x, y, z - s, c) for s in REL[1:]]
-    partners += [device(x + s, y, z, c) for s in (1, 2, 3)]
-    for partner in partners:
-        pl.semaphore_signal(barrier, inc=1, device_id=partner, device_id_type=MESH)
 
     msg[...] = jnp.zeros_like(msg)
     for number in range(2):
@@ -253,20 +253,16 @@
     after_z(2)
     after_y(1)
     after_z(3)
+    after_y(2)
     after_far(0)
-    after_z(4)
-    after_y(2)
     after_far(1)
     after_y(3)
-    after_y(4)
-    after_far(2)
     after_x(0)
     after_x(1)
+    after_far(2)
+    after_x(2)
     after_far(3)
-    after_far(4)
-    after_x(2)
     after_x(3)
-    after_x(4)
 
     def weights(dy, base, half):
         t0 = held[c, half, :, :, base + 16 * dy : base + 16 * dy + 16].reshape(512, 128)

time: 38.2 us -> 37.6 us (0.984)
  Pallas kernels: 37.4 us -> 36.8 us
    pallas_call x1, Pallas kernels: 37.4 us -> 36.8 us  [shards(): pl.pallas_call(kernel, out_shape=jax.ShapeDtypeStruct((2, 320, 128), BF),...]
where the time goes in v4:
time: 37.6 us; the launch traced here: 37.5 us
  Pallas kernels  36.8 us (98%)
  local copies, waits for them, and re-layouts  0.67 us (2%)
    pallas_call x1, Pallas kernels, shards(): pl.pallas_call(kernel, out_shape=jax.ShapeDtypeStruct((2, 320, 128), BF),...  36.8 us

profile of v4, /device:TPU:1, one launch (start us, length us, event | category | flops | bytes accessed | tf_op | source)
XLA Modules:
  0.0 37.5 jit_solution(18354123966052726823)
XLA Ops:
  0.0 36.8 %residual_block.1 = bf16[2,320,128]{2,1,0:T(8,128)(2,1)S(1)} custom-call(bf16[2,320,128]{2,1,0:T(8,128)(2,1)} %bitcast.9, f32[1,32]{1,0:T(1,128)} %mean1.1, f32[1,32]{1,0:T(1,128)} %rstd1.1, f32[320]{0:T(512)} %gain1.1, f32[320]{0:T(512)} %shift1.1, bf16[9,4,200]{2,1,0:T(4,128)(2,1)} %bitcast.10, f32[320]{0:T(512)} %bias1.1, f32[1,320]{1,0:T(1,128)} %embed.1, ...), custom_call_target="tpu_custom_call" | custom-call | tf_op jit(solution)/shard_map/residual_block/pallas_call | solution.py:312
  36.8 0.7 %copy.16 = bf16[1,2,128,320]{2,3,1,0:T(8,128)(2,1)} copy(bf16[1,2,128,320]{2,3,1,0:T(8,128)(2,1)S(1)} %bitcast.8) | data formatting | bytes 327680

commit v5 on v4

--- a/solution.py
+++ b/solution.py
@@ -13,7 +13,9 @@
 REL = (0, 1, -1, 2, -2, 3, -3, 4)
 CHUNKS = ((0, 1), (1, 3), (3, 5), (5, 8))
 Z_ORDER = (1, 2, 3, 4, 5, 6, 7)
-FAR = ()
+FAR = (0,)
+ACROSS = (1,)
+TURNED = (1, 2, 3)
 COPIES = 64
 SWAPS = tuple((a, b) for a in range(4) for b in range(2) if (a, b) != (0, 0))
 SLOT = 128
@@ -191,6 +193,7 @@
         low, high = chunk
         return held.at[core, xr, yr, pl.ds(low, high - low)]
 
+    turned = {}
     z_copies, y_copies, far_copies, x_copies, core_copies = {}, {}, {}, {}, ({}, {})
 
     def send_z():
@@ -223,24 +226,51 @@
         chunk = CHUNKS[k]
         from_up, from_down = y_copies[k]
         from_up.wait_recv()
-        if k % 2 and k not in FAR:
+        if k % 2 and k not in FAR + TURNED:
             far_copies[k] = send(at(0, 1, chunk), at(0, 3, chunk), down)
-        send_x(k, 1)
+        if k not in ACROSS:
+            send_x(k, 1)
         from_down.wait_recv()
-        if k % 2 == 0 and k not in FAR:
+        if k % 2 == 0 and k not in FAR + TURNED:
             far_copies[k] = send(at(0, 2, chunk), at(0, 3, chunk), up)
 
+    def turn():
+        for i in Z_ORDER:
+            back = REL.index(-REL[i]) if REL[i] != 4 else 7
+            if any(CHUNKS[k][0] <= back < CHUNKS[k][1] for k in TURNED):
+                turned[back] = send(at(0, 3, (0, 1)), at(0, 3, (back, back + 1)), device(x, y, z + REL[i], c))
+
     def after_far(k):
-        far_copies[k].wait_recv()
+        if k in TURNED:
+            for i in range(*CHUNKS[k]):
+                turned[i].wait_recv()
+        else:
+            far_copies[k].wait_recv()
+        if k == 0:
+            turn()
         send_core(k, 0)
 
+    def wait_x(k, base):
+        for side in range(2):
+            ref = at(1, 0, CHUNKS[k])
+            pltpu.make_async_remote_copy(
+                src_ref=ref, dst_ref=ref, send_sem=sent.at[0], recv_sem=landed.at[base + side],
+                device_id=right, device_id_type=MESH).wait_recv()
+
+    crossed = {}
+
+    def cross(k):
+        chunk = CHUNKS[k]
+        wait_x(k, x_copies[k][0])
+        crossed[k] = send(at(1, 0, chunk), at(1, 1, chunk), down), send(at(1, 0, chunk), at(1, 3, chunk), up)
+
     def after_x(k):
-        for base in x_copies[k]:
-            for side in range(2):
-                ref = at(1, 0, CHUNKS[k])
-                pltpu.make_async_remote_copy(
-                    src_ref=ref, dst_ref=ref, send_sem=sent.at[0], recv_sem=landed.at[base + side],
-                    device_id=right, device_id_type=MESH).wait_recv()
+        if k in ACROSS:
+            for copy in crossed[k]:
+                copy.wait_recv()
+        else:
+            for base in x_copies[k]:
+                wait_x(k, base)
         send_core(k, 1)
 
     send_z()
@@ -249,15 +279,16 @@
     activate(1 - h, 0)
     after_z(1)
     after_y(0)
+    after_far(0)
     activate(1 - h, 1)
     after_z(2)
     after_y(1)
     after_z(3)
+    cross(1)
     after_y(2)
-    after_far(0)
     after_far(1)
+    after_x(0)
     after_y(3)
-    after_x(0)
     after_x(1)
     after_far(2)
     after_x(2)

time: 37.6 us -> 36.5 us (0.971)
  Pallas kernels: 36.8 us -> 35.8 us
    pallas_call x1, Pallas kernels: 36.8 us -> 35.8 us  [shards(): pl.pallas_call(kernel, out_shape=jax.ShapeDtypeStruct((2, 320, 128), BF),...]
where the time goes in v5:
time: 36.5 us; the launch traced here: 36.4 us
  Pallas kernels  35.8 us (98%)
  local copies, waits for them, and re-layouts  0.67 us (2%)
    pallas_call x1, Pallas kernels, shards(): pl.pallas_call(kernel, out_shape=jax.ShapeDtypeStruct((2, 320, 128), BF),...  35.8 us

profile of v5, /device:TPU:1, one launch (start us, length us, event | category | flops | bytes accessed | tf_op | source)
XLA Modules:
  0.0 36.4 jit_solution(7394925724869263596)
XLA Ops:
  0.0 35.8 %residual_block.1 = bf16[2,320,128]{2,1,0:T(8,128)(2,1)S(1)} custom-call(bf16[2,320,128]{2,1,0:T(8,128)(2,1)} %bitcast.9, f32[1,32]{1,0:T(1,128)} %mean1.1, f32[1,32]{1,0:T(1,128)} %rstd1.1, f32[320]{0:T(512)} %gain1.1, f32[320]{0:T(512)} %shift1.1, bf16[9,4,200]{2,1,0:T(4,128)(2,1)} %bitcast.10, f32[320]{0:T(512)} %bias1.1, f32[1,320]{1,0:T(1,128)} %embed.1, ...), custom_call_target="tpu_custom_call" | custom-call | tf_op jit(solution)/shard_map/residual_block/pallas_call | solution.py:343
  35.8 0.7 %copy.16 = bf16[1,2,128,320]{2,3,1,0:T(8,128)(2,1)} copy(bf16[1,2,128,320]{2,3,1,0:T(8,128)(2,1)S(1)} %bitcast.8) | data formatting | bytes 327680

commit v6 on v5

--- a/solution.py
+++ b/solution.py
@@ -92,6 +92,10 @@
 
     pl.semaphore_wait(barrier, len(partners))
 
+    lat_copy = pltpu.make_async_remote_copy(
+        src_ref=lat_ref, dst_ref=lat.at[h], send_sem=lat_send, recv_sem=lat_recv,
+        device_id=device(x + 2, y, z, c), device_id_type=MESH)
+    lat_copy.start()
     swaps = []
     q = 2 * y + c
     for i, (a, b) in enumerate(SWAPS):
@@ -100,10 +104,6 @@
             device_id=device(x, y + a, z, c + b), device_id_type=MESH)
         copy.start()
         swaps.append(copy)
-    lat_copy = pltpu.make_async_remote_copy(
-        src_ref=lat_ref, dst_ref=lat.at[h], send_sem=lat_send, recv_sem=lat_recv,
-        device_id=device(x + 2, y, z, c), device_id_type=MESH)
-    lat_copy.start()
     got[q] = msg[(y + 2 * h) % 4]
 
     lane = lax.broadcasted_iota(jnp.int32, (1, 1024), 1)

time: 36.5 us -> 36.5 us (level)
  no operation moved by 1% of the time
where the time goes in v6:
time: 36.5 us
  Pallas kernels  35.8 us (98%)
  local copies, waits for them, and re-layouts  0.67 us (2%)
    pallas_call x1, Pallas kernels, shards(): pl.pallas_call(kernel, out_shape=jax.ShapeDtypeStruct((2, 320, 128), BF),...  35.8 us

profile of v6, /device:TPU:1, one launch (start us, length us, event | category | flops | bytes accessed | tf_op | source)
XLA Modules:
  0.0 36.5 jit_solution(6677054094982081285)
XLA Ops:
  0.0 35.8 %residual_block.1 = bf16[2,320,128]{2,1,0:T(8,128)(2,1)S(1)} custom-call(bf16[2,320,128]{2,1,0:T(8,128)(2,1)} %bitcast.9, f32[1,32]{1,0:T(1,128)} %mean1.1, f32[1,32]{1,0:T(1,128)} %rstd1.1, f32[320]{0:T(512)} %gain1.1, f32[320]{0:T(512)} %shift1.1, bf16[9,4,200]{2,1,0:T(4,128)(2,1)} %bitcast.10, f32[320]{0:T(512)} %bias1.1, f32[1,320]{1,0:T(1,128)} %embed.1, ...), custom_call_target="tpu_custom_call" | custom-call | tf_op jit(solution)/shard_map/residual_block/pallas_call | solution.py:343
  35.8 0.7 %copy.16 = bf16[1,2,128,320]{2,3,1,0:T(8,128)(2,1)} copy(bf16[1,2,128,320]{2,3,1,0:T(8,128)(2,1)S(1)} %bitcast.8) | data formatting | bytes 327680
